TPU v7x, 512 devices: a whole 4x8x8 slice. The times are simulated.
512 devices in a mesh: section: 4 (over x), seq: 128 (over z, y, core).
Axes of the slice: x: 4, y: 8, z: 8, core: 2. Of those that a mesh axis runs over, the one named last changes fastest.
Arguments:
- hidden: bfloat16 [65536, 4096], P('seq', 'section'), may hold values from -6 to 6
- norm_gain: bfloat16 [4096], P('section'), may hold values from 0.25 to 1.75
- query_weight: bfloat16 [4096, 512], P(None, 'section')
- key_weight: bfloat16 [4096, 128], P('section')
- value_weight: bfloat16 [4096, 128], P('section'), may hold values from -0.5 to 0.5
- output_weight: bfloat16 [512, 4096], P(None, 'section'), may hold values from -0.25 to 0.25
- block_reach: int32 [512], P('seq'), may hold values from 0 to 2
- header_ids: int32 [2], replicated, may hold values from 0 to 511, as said below
Outputs:
- attention_out: bfloat16 [65536, 4096], P('seq', 'section')
Inputs may be any that keep to these rules, and one draw needn't show every extreme that they name: `header_ids`: the 2 indices are distinct block indices, and the last block, 511, is always one of them, at any position.
All inputs are finite; a program needn't handle non-finite values.
Results may differ from a plain program's by a relative error of at most 0.014.
Values may be sent and summed in bfloat16 or wider, within the bound.
No kernel may reach another device: no remote copies, remote signals or barrier semaphores. Data moves between devices by JAX's collectives and lax.ppermute only.
A program may use at most 64 MiB of HBM per device.

v0:
```python
import math
import jax
import jax.numpy as jnp
from jax import lax
from jax.sharding import PartitionSpec as P

BLOCK = 128
REACH = 2
EPSILON = 1e-05
THETA = 500000.0


def shift(value, axis, by):
    count = lax.axis_size(axis)
    return lax.ppermute(value, axis, [(i, (i + by) % count) for i in range(count)])


def tables(positions, head_width):
    middle = head_width // 2
    frequency = jnp.exp(
        -(2.0 / head_width) * math.log(THETA) * jnp.arange(middle, dtype=jnp.float32)
    )
    angles = positions.astype(jnp.float32)[:, None] * frequency[None, :]
    cosine, sine = (jnp.cos(angles), jnp.sin(angles))
    return (jnp.concatenate([cosine, cosine], axis=1), jnp.concatenate([-sine, sine], axis=1))


def rotate(values, cosine, signed_sine):
    middle = values.shape[-1] // 2
    turned = jnp.concatenate([values[..., middle:], values[..., :middle]], axis=-1)
    return values * cosine + turned * signed_sine


def project(total, cosine, sine, head_width):
    bf16 = jnp.bfloat16
    queries = rotate(total[:, :head_width], cosine, sine).astype(bf16)
    keys = rotate(total[:, head_width : 2 * head_width], cosine, sine).astype(bf16)
    return (queries, keys, total[:, 2 * head_width :].astype(bf16))


def on_device(
    hidden,
    norm_gain,
    query_weight,
    key_weight,
    value_weight,
    output_weight,
    block_reach,
    header_ids,
):
    bf16, f32 = (jnp.bfloat16, jnp.float32)
    rows, part = hidden.shape
    head_width = key_weight.shape[1]
    sections = lax.axis_size("section")
    shards = lax.axis_size("seq")
    local_blocks = rows // BLOCK
    total_blocks = local_blocks * shards
    section_place = lax.axis_index("section")
    seq_place = lax.axis_index("seq")
    headers = header_ids.shape[0]
    lines = BLOCK // shards
    mine = headers * lines
    owners = header_ids // local_blocks
    slots = header_ids % local_blocks
    width = part * sections
    gain = norm_gain.astype(f32)[None, :]
    candidates = jnp.concatenate(
        [
            lax.dynamic_slice_in_dim(hidden, slots[h] * BLOCK, BLOCK, axis=0).reshape(
                shards, lines, part
            )
            for h in range(headers)
        ],
        axis=1,
    )
    spread = lax.all_to_all(candidates, "seq", 0, 0)
    floats = hidden.astype(f32)
    squares = jnp.sum(floats * floats, axis=1).reshape(-1, head_width)
    squares_high = squares.astype(bf16)
    squares_low = (squares - squares_high.astype(f32)).astype(bf16)
    square_rows = squares.shape[0]
    head_weights = []
    for k in range(sections):
        target = (section_place + k) % sections
        piece = lax.dynamic_slice_in_dim(query_weight, target * part, part, axis=0)
        if k:
            piece = jnp.concatenate([piece, squares_high, squares_low])
            piece = shift(piece, "section", k)
            tail = piece[part:].astype(f32)
            squares = squares + tail[:square_rows] + tail[square_rows:]
            piece = piece[:part]
        head_weights.append(piece)
    scaling = lax.rsqrt(squares.reshape(-1) / width + EPSILON)
    normed = (floats * scaling[:, None] * gain).astype(bf16)
    header_rows = jnp.concatenate(
        [
            lax.dynamic_slice_in_dim(spread, owners[h], 1, axis=0)[0, h * lines : (h + 1) * lines]
            for h in range(headers)
        ]
    ).astype(f32)
    gained = header_rows * gain
    gained_high = gained.astype(bf16)
    gained_low = (gained - gained_high.astype(f32)).astype(bf16)
    left = jnp.concatenate([normed, gained_high, gained_low])
    header_squares = jnp.broadcast_to(
        jnp.sum(header_rows * header_rows, axis=1, keepdims=True), (mine, head_width)
    )
    products = [
        jnp.dot(left, weight, preferred_element_type=f32)
        for weight in head_weights + [key_weight, value_weight]
    ]
    mains = [value[:rows].astype(bf16) for value in products]
    smalls = [value[rows : rows + mine] + value[rows + mine :] for value in products]
    highs = [value.astype(bf16) for value in smalls + [header_squares]]
    lows = [
        (value - high.astype(f32)).astype(bf16)
        for value, high in zip(smalls + [header_squares], highs)
    ]
    used = 3 * rows + 8 * mine
    filler = jnp.zeros((-used % BLOCK, head_width), bf16)
    chunks = []
    for target in range(sections):
        which = (section_place - target) % sections

        def chosen(options):
            value = options[0]
            for k in range(1, sections):
                value = jnp.where(which == k, options[k], value)
            return value

        chunks.append(
            jnp.concatenate(
                [chosen(mains), mains[sections], mains[sections + 1]]
                + [chosen(highs)]
                + highs[sections:]
                + [chosen(lows)]
                + lows[sections:]
                + [filler]
            )
        )
    arrived = lax.all_to_all(jnp.stack(chunks), "section", 0, 0)
    total = jnp.sum(arrived[:, :used].astype(f32), axis=0)
    small = total[3 * rows :]
    small = (small[: 4 * mine] + small[4 * mine :]).reshape(4, mine, head_width)
    small = small[:3] * lax.rsqrt(small[3] / width + EPSILON)
    total = jnp.concatenate([total[k * rows : (k + 1) * rows] for k in range(3)], axis=1)
    header_total = jnp.concatenate([small[0], small[1], small[2]], axis=1)
    header_positions = (
        header_ids[:, None] * BLOCK + seq_place * lines + jnp.arange(lines, dtype=jnp.int32)[None]
    ).reshape(-1)
    header_chunk = jnp.concatenate(
        project(header_total, *tables(header_positions, head_width), head_width), axis=1
    )
    header_pack = lax.all_to_all(
        jnp.broadcast_to(header_chunk[None], (shards,) + header_chunk.shape), "seq", 0, 0
    ).reshape(-1, 3 * head_width)
    own_positions = seq_place * rows + jnp.arange(rows, dtype=jnp.int32)
    queries, keys, values = project(total, *tables(own_positions, head_width), head_width)
    stacked = jnp.concatenate([keys, values], axis=1)
    head_queries = header_pack[:, :head_width]
    head_keys = header_pack[:, head_width : 2 * head_width]
    head_values = header_pack[:, 2 * head_width :]
    inverse_root = 1.0 / math.sqrt(head_width)
    far_scores = (
        jnp.einsum("qd,kd->qk", head_queries, keys, preferred_element_type=f32) * inverse_root
    )
    far_max = jnp.max(far_scores, axis=1, keepdims=True)
    far_weights = jnp.exp(far_scores - far_max)
    far_total = jnp.sum(far_weights, axis=1, keepdims=True)
    far_out = jnp.dot(far_weights.astype(bf16), values, preferred_element_type=f32) / far_total
    far_level = far_max + jnp.log(far_total)
    first = far_level.astype(bf16).astype(f32)
    second = (far_level - first).astype(bf16).astype(f32)
    third = far_level - first - second
    lane = lax.broadcasted_iota(jnp.int32, far_out.shape, 1)
    level = jnp.where(lane < 32, first, jnp.where(lane < 64, second, third))
    partial = jnp.concatenate([far_out, level], axis=1).astype(bf16)
    partial, queries = lax.optimization_barrier((partial, queries))
    parts = lax.all_to_all(partial.reshape(shards, mine, 2 * head_width), "seq", 0, 0)
    parts = parts.astype(f32)
    levels = sum((parts[..., head_width + lane : head_width + lane + 1] for lane in (0, 32, 64)))
    factor = jnp.exp(levels - jnp.max(levels, axis=0, keepdims=True))
    header_result = jnp.sum(parts[..., :head_width] * factor, axis=0) / jnp.sum(factor, axis=0)
    header_all = lax.all_to_all(
        jnp.broadcast_to(header_result.astype(bf16)[None], (shards, mine, head_width)), "seq", 0, 0
    ).reshape(shards, headers, lines, head_width)
    margin_rows = REACH * BLOCK
    extended = jnp.concatenate(
        [
            shift(stacked[rows - margin_rows :], "seq", 1),
            stacked,
            shift(stacked[:margin_rows], "seq", -1),
        ]
    )
    near_keys = extended[:, :head_width]
    near_values = extended[:, head_width:]
    extent = rows + 2 * margin_rows
    key_blocks = seq_place * local_blocks - REACH + jnp.arange(extent, dtype=jnp.int32) // BLOCK
    query_blocks = seq_place * local_blocks + jnp.arange(rows, dtype=jnp.int32) // BLOCK
    limits = jnp.repeat(block_reach, BLOCK)
    key_header = jnp.any(header_ids[:, None] == key_blocks[None, :], axis=0)
    allowed = (key_blocks >= 0)[None, :] & (key_blocks < total_blocks)[None, :]
    allowed = allowed & (jnp.abs(key_blocks[None, :] - query_blocks[:, None]) <= limits[:, None])
    allowed = allowed & jnp.logical_not(key_header)[None, :]
    near_scores = (
        jnp.einsum("qd,kd->qk", queries, near_keys, preferred_element_type=f32) * inverse_root
    )
    near_scores = jnp.where(allowed, near_scores, -jnp.inf)
    head_scores = (
        jnp.einsum("qd,kd->qk", queries, head_keys, preferred_element_type=f32) * inverse_root
    )
    scores = jnp.concatenate([near_scores, head_scores], axis=1)
    row_top = jnp.max(scores, axis=1)
    weights = jnp.exp(scores - row_top[:, None])
    row_sums = jnp.sum(weights, axis=1)
    joined = jnp.concatenate([near_values, head_values], axis=0)
    mixed = (
        jnp.dot(weights.astype(bf16), joined, preferred_element_type=f32) / row_sums[:, None]
    ).astype(bf16)
    blocks = []
    for b in range(local_blocks):
        block = mixed[b * BLOCK : (b + 1) * BLOCK]
        for h in range(headers):
            here = header_ids[h] == seq_place * local_blocks + b
            block = jnp.where(here, header_all[:, h].reshape(BLOCK, head_width), block)
        blocks.append(block)
    attended = jnp.concatenate(blocks, axis=0)
    gathered = lax.all_gather(attended, "section", axis=1, tiled=True)
    return jnp.dot(gathered, output_weight, preferred_element_type=f32).astype(bf16)


def solution(mesh):
    return jax.shard_map(
        on_device,
        mesh=mesh,
        in_specs=(
            P("seq", "section"),
            P("section"),
            P(None, "section"),
            P("section", None),
            P("section", None),
            P(None, "section"),
            P("seq"),
            P(),
        ),
        out_specs=P("seq", "section"),
        check_vma=False,
    )
```

profile of v0, /device:TPU:2, one launch (start us, length us, event | category | flops | bytes accessed | tf_op | source)
XLA Modules:
  0.0 179.3 jit_solution(14884136693440306708)
XLA Ops:
  0.1 1.6 fusion.1
  1.7 1.2 constant_dynamic-slice_fusion.2
  3.0 7.8 %collective-permute-start.2 = (bf16[1032,128]{1,0:T(8,128)(2,1)S(1)}, bf16[1032,128]{1,0:T(8,128)(2,1)}, u32[]{:S(2)}, u32[]{:S(2)}) collective-permute-start(bf16[1032,128]{1,0:T(8,128)(2,1)S(1)} %concatenate.78), channel_id=1, source_target_pairs={{0,384},{128,0},{256,128},{384,256},{1,385},{129,1},{257,129},{385... | collective-permute-start | bytes 792584 | tf_op jit(solution)/shard_map/ppermute | solution.py:15
  11.0 1.9 %collective-permute-start.1 = (bf16[1032,128]{1,0:T(8,128)(2,1)S(1)}, bf16[1032,128]{1,0:T(8,128)(2,1)}, u32[]{:S(2)}, u32[]{:S(2)}) collective-permute-start(bf16[1032,128]{1,0:T(8,128)(2,1)S(1)} %concatenate.77), channel_id=1, source_target_pairs={{0,256},{128,384},{256,0},{384,128},{1,257},{129,385},{257,1},{385... | collective-permute-start | bytes 792584 | tf_op jit(solution)/shard_map/ppermute | solution.py:15
  15.3 1.3 copy.27
  16.7 15.4 %all-to-all-start = ((bf16[128,2,1024]{2,1,0:T(2,128)(2,1)}), bf16[128,2,1024]{2,1,0:T(2,128)(2,1)}, u32[]{:S(2)}, u32[]{:S(2)}) async-start(bf16[128,2,1024]{2,1,0:T(2,128)(2,1)} %copy.27), calls=%async_computation | async-start | bytes 1048576 | tf_op jit(solution)/shard_map/all_to_all | solution.py:76
  32.2 3.7 %collective-permute-start = (bf16[1032,128]{1,0:T(8,128)(2,1)S(1)}, bf16[1032,128]{1,0:T(8,128)(2,1)}, u32[]{:S(2)}, u32[]{:S(2)}) collective-permute-start(bf16[1032,128]{1,0:T(8,128)(2,1)S(1)} %concatenate.76), channel_id=1, source_target_pairs={{0,128},{128,256},{256,384},{384,0},{1,129},{129,257},{257,385},{3... | collective-permute-start | bytes 792584 | tf_op jit(solution)/shard_map/ppermute | solution.py:15
  39.5 0.7 slice_convert_fusion.7
  40.2 0.7 slice_convert_fusion.8
  40.9 1.1 collective-permute-done
  42.0 0.7 slice_convert_fusion.9
  43.0 7.9 %all-to-all-done = bf16[128,2,1024]{2,1,0:T(2,128)(2,1)} async-done(((bf16[128,2,1024]{2,1,0:T(2,128)(2,1)}), bf16[128,2,1024]{2,1,0:T(2,128)(2,1)}, u32[]{:S(2)}, u32[]{:S(2)}) %all-to-all-start) | async-done | bytes 524320 | tf_op jit(solution)/shard_map/all_to_all | solution.py:76
  50.9 0.7 dynamic-slice_bitcast_fusion.3
  51.8 1.4 fusion.35
  53.2 1.4 fusion.28
  54.6 1.4 fusion.30
  56.0 1.4 fusion.32
  59.9 1.4 pad_maximum_fusion
  61.4 5.3 %all-to-all-start.1 = ((bf16[4,1664,128]{2,1,0:T(8,128)(2,1)}), bf16[4,1664,128]{2,1,0:T(8,128)(2,1)S(1)}, u32[]{:S(2)}, u32[]{:S(2)}) async-start(bf16[4,1664,128]{2,1,0:T(8,128)(2,1)} %pad_maximum_fusion), calls=%async_computation.1 | async-start | bytes 3407872 | tf_op jit(solution)/shard_map/all_to_all | solution.py:141
  67.8 0.7 compare_reduce_fusion
  69.1 0.7 fusion.84
  69.8 1.9 %fusion.39 = (f32[512,64]{1,0:T(8,128)}, f32[512,64]{1,0:T(8,128)}, f32[512,64]{1,0:T(8,128)}) fusion(f32[64]{0:T(128)S(1)} %multiply_exponential_fusion, f32[512]{0:T(512)S(1)} %add_convert_fusion), kind=kLoop, calls=%fused_computation.79 | loop fusion | flops 65536 | bytes 395520 | tf_op jit(solution)/shard_map/neg | solution.py:25
  71.7 16.7 %all-to-all-done.1 = bf16[4,1664,128]{2,1,0:T(8,128)(2,1)S(1)} async-done(((bf16[4,1664,128]{2,1,0:T(8,128)(2,1)}), bf16[4,1664,128]{2,1,0:T(8,128)(2,1)S(1)}, u32[]{:S(2)}, u32[]{:S(2)}) %all-to-all-start.1) | async-done | bytes 1703968 | tf_op jit(solution)/shard_map/all_to_all | solution.py:141
  88.7 0.9 fusion.95
  89.8 0.8 fusion.70
  90.7 0.8 broadcast_in_dim.42
  91.4 7.2 %all-to-all-start.2 = ((bf16[128,2,384]{2,1,0:T(2,128)(2,1)}), bf16[128,2,384]{2,1,0:T(2,128)(2,1)}, u32[]{:S(2)}, u32[]{:S(2)}) async-start(bf16[128,2,384]{2,1,0:T(2,128)(2,1)} %broadcast_in_dim.42), calls=%async_computation.2 | async-start | bytes 393216 | tf_op jit(solution)/shard_map/all_to_all | solution.py:154
  98.7 1.4 fusion.25
  100.1 6.8 %collective-permute-start.4 = (bf16[256,256]{1,0:T(8,128)(2,1)S(1)}, bf16[256,256]{1,0:T(8,128)(2,1)S(1)}, u32[]{:S(2)}, u32[]{:S(2)}) collective-permute-start(bf16[256,256]{1,0:T(8,128)(2,1)S(1)} %get-tuple-element.52), channel_id=1, source_target_pairs={{0,127},{1,0},{2,1},{3,2},{4,3},{5,4},{6,5},{7,6},{8,7},{9,8},{10,... | collective-permute-start | bytes 393224 | tf_op jit(solution)/shard_map/ppermute | solution.py:15
  106.9 2.1 %collective-permute-start.3 = (bf16[256,256]{1,0:T(8,128)(2,1)S(1)}, bf16[256,256]{1,0:T(8,128)(2,1)S(1)}, u32[]{:S(2)}, u32[]{:S(2)}) collective-permute-start(bf16[256,256]{1,0:T(8,128)(2,1)S(1)} %get-tuple-element.51), channel_id=1, source_target_pairs={{0,1},{1,2},{2,3},{3,4},{4,5},{5,6},{6,7},{7,8},{8,9},{9,10},{10,1... | collective-permute-start | bytes 393224 | tf_op jit(solution)/shard_map/ppermute | solution.py:15
  113.7 0.7 not.7
  114.4 2.1 %collective-permute-done.3 = bf16[256,256]{1,0:T(8,128)(2,1)S(1)} collective-permute-done((bf16[256,256]{1,0:T(8,128)(2,1)S(1)}, bf16[256,256]{1,0:T(8,128)(2,1)S(1)}, u32[]{:S(2)}, u32[]{:S(2)}) %collective-permute-start.3) | collective-permute-done | bytes 131104 | tf_op jit(solution)/shard_map/ppermute | solution.py:15
  116.6 0.8 copy-done.3
  117.4 0.7 slice.376
  118.1 1.0 reshape.162
  120.2 0.7 reshape.163
  120.9 8.7 %all-to-all-start.3 = ((bf16[128,2,256]{2,1,0:T(2,128)(2,1)}), bf16[128,2,256]{2,1,0:T(2,128)(2,1)}, u32[]{:S(2)}, u32[]{:S(2)}) async-start(bf16[128,2,256]{2,1,0:T(2,128)(2,1)} %reshape.163), calls=%async_computation.3 | async-start | bytes 262144 | tf_op jit(solution)/shard_map/all_to_all | solution.py:179
  129.7 2.0 %fusion.102 = (f32[512]{0:T(512)S(1)}, f32[512,1024]{1,0:T(8,128)S(1)}) fusion(bf16[512,128]{1,0:T(8,128)(2,1)S(1)} %get-tuple-element.8, bf16[1024,256]{1,0:T(8,128)(2,1)} %copy-done.3, pred[1024]{0:T(1024)(128)(4,1)S(1)} %not.7, s32[512]{0:T(512)S(1)} %copy-done.11, s32[512]{0:T(512)S(1)} %fusion.54, s32[1024]{0:T(1024)S(1)} %fusion.50, ...), kind=kOutput, calls=%fused_computation.232 | convolution fusion | flops 138411520 | bytes 2502656 | tf_op jit(solution)/shard_map/qd,kd->qk/dot_general | solution.py:206
  132.0 0.8 copy-done.2
  133.3 8.1 %all-to-all-done.3 = bf16[128,2,256]{2,1,0:T(2,128)(2,1)} async-done(((bf16[128,2,256]{2,1,0:T(2,128)(2,1)}), bf16[128,2,256]{2,1,0:T(2,128)(2,1)}, u32[]{:S(2)}, u32[]{:S(2)}) %all-to-all-start.3) | async-done | bytes 131104 | tf_op jit(solution)/shard_map/all_to_all | solution.py:179
  141.4 1.0 convert_element_type.263
  142.9 0.9 fusion.87
  143.8 1.0 copy.29
  145.9 6.1 %all-to-all-start.4 = ((bf16[128,2,128]{2,1,0:T(2,128)(2,1)}), bf16[128,2,128]{2,1,0:T(2,128)(2,1)S(1)}, u32[]{:S(2)}, u32[]{:S(2)}) async-start(bf16[128,2,128]{2,1,0:T(2,128)(2,1)} %broadcast_in_dim.46), calls=%async_computation.4 | async-start | bytes 131072 | tf_op jit(solution)/shard_map/all_to_all | solution.py:184
  152.0 1.7 fusion.13
  153.7 9.4 %all-to-all-done.4 = bf16[128,2,128]{2,1,0:T(2,128)(2,1)S(1)} async-done(((bf16[128,2,128]{2,1,0:T(2,128)(2,1)}), bf16[128,2,128]{2,1,0:T(2,128)(2,1)S(1)}, u32[]{:S(2)}, u32[]{:S(2)}) %all-to-all-start.4) | async-done | bytes 65568 | tf_op jit(solution)/shard_map/all_to_all | solution.py:184
  163.2 14.4 %all_gather.3 = bf16[512,512]{1,0:T(8,128)(2,1)S(1)} all-gather(bf16[512,128]{1,0:T(8,128)(2,1)S(1)} %pad_maximum_fusion.8), channel_id=1, replica_groups=mesh['section'=4,'seq'=128] {'section'}, dimensions={1}, use_global_device_ids=true | all-gather | bytes 655360 | tf_op jit(solution)/shard_map/all_gather | solution.py:228
  177.6 1.7 convolution_convert_fusion
  (113 shorter events, 10.4 us)
Async XLA Ops:
  0.0 177.6 %copy-start = (bf16[512,1024]{1,0:T(8,128)(2,1)S(1)}, bf16[512,1024]{1,0:T(8,128)(2,1)}, u32[]{:S(2)}) copy-start(bf16[512,1024]{1,0:T(8,128)(2,1)} %param.13) | copy-start | bytes 3145732
  0.0 15.2 %copy-start.1 = (bf16[512,1024]{1,0:T(8,128)(2,1)S(1)}, bf16[512,1024]{1,0:T(8,128)(2,1)}, u32[]{:S(2)}) copy-start(bf16[512,1024]{1,0:T(8,128)(2,1)} %param.8) | copy-start | bytes 3145732
  0.0 12.9 %copy-start.9 = (s32[2]{0:T(128)S(1)}, s32[2]{0:T(128)}, u32[]{:S(2)}) copy-start(s32[2]{0:T(128)} %param.15) | copy-start | bytes 28
  3.0 36.5 %collective-permute-start.2 = (bf16[1032,128]{1,0:T(8,128)(2,1)S(1)}, bf16[1032,128]{1,0:T(8,128)(2,1)}, u32[]{:S(2)}, u32[]{:S(2)}) collective-permute-start(bf16[1032,128]{1,0:T(8,128)(2,1)S(1)} %concatenate.78), channel_id=1, source_target_pairs={{0,384},{128,0},{256,128},{384,256},{1,385},{129,1},{257,129},{385... | collective-permute-start | bytes 792584 | tf_op jit(solution)/shard_map/ppermute | solution.py:15
  11.0 29.2 %collective-permute-start.1 = (bf16[1032,128]{1,0:T(8,128)(2,1)S(1)}, bf16[1032,128]{1,0:T(8,128)(2,1)}, u32[]{:S(2)}, u32[]{:S(2)}) collective-permute-start(bf16[1032,128]{1,0:T(8,128)(2,1)S(1)} %concatenate.77), channel_id=1, source_target_pairs={{0,256},{128,384},{256,0},{384,128},{1,257},{129,385},{257,1},{385... | collective-permute-start | bytes 792584 | tf_op jit(solution)/shard_map/ppermute | solution.py:15
  15.3 23.1 %copy-start.10 = (bf16[1024]{0:T(1024)(128)(2,1)S(1)}, bf16[1024]{0:T(1024)(128)(2,1)}, u32[]{:S(2)}) copy-start(bf16[1024]{0:T(1024)(128)(2,1)} %param.9) | copy-start | bytes 6148
  16.7 34.3 %all-to-all-start = ((bf16[128,2,1024]{2,1,0:T(2,128)(2,1)}), bf16[128,2,1024]{2,1,0:T(2,128)(2,1)}, u32[]{:S(2)}, u32[]{:S(2)}) async-start(bf16[128,2,1024]{2,1,0:T(2,128)(2,1)} %copy.27), calls=%async_computation | async-start | bytes 1048576 | tf_op jit(solution)/shard_map/all_to_all | solution.py:76
  32.2 9.8 %collective-permute-start = (bf16[1032,128]{1,0:T(8,128)(2,1)S(1)}, bf16[1032,128]{1,0:T(8,128)(2,1)}, u32[]{:S(2)}, u32[]{:S(2)}) collective-permute-start(bf16[1032,128]{1,0:T(8,128)(2,1)S(1)} %concatenate.76), channel_id=1, source_target_pairs={{0,128},{128,256},{256,384},{384,0},{1,129},{129,257},{257,385},{3... | collective-permute-start | bytes 792584 | tf_op jit(solution)/shard_map/ppermute | solution.py:15
  56.0 1.6 copy-start.16
  57.6 1.0 copy-start.17
  61.4 7.1 %copy-start.15 = (s32[4]{0:T(128)S(1)}, s32[4]{0:T(128)}, u32[]{:S(2)}) copy-start(s32[4]{0:T(128)} %param.14) | copy-start | bytes 52
  61.4 7.8 %copy-start.12 = (f32[2]{0:T(128)S(1)}, f32[2]{0:T(128)}, u32[]{:S(2)}) copy-start(f32[2]{0:T(128)} %get-tuple-element.83) | copy-start | bytes 28
  61.4 27.0 %all-to-all-start.1 = ((bf16[4,1664,128]{2,1,0:T(8,128)(2,1)}), bf16[4,1664,128]{2,1,0:T(8,128)(2,1)S(1)}, u32[]{:S(2)}, u32[]{:S(2)}) async-start(bf16[4,1664,128]{2,1,0:T(8,128)(2,1)} %pad_maximum_fusion), calls=%async_computation.1 | async-start | bytes 3407872 | tf_op jit(solution)/shard_map/all_to_all | solution.py:141
  88.6 10.0 %copy-start.4 = (f32[512,64]{1,0:T(8,128)S(1)}, f32[512,64]{1,0:T(8,128)}, u32[]{:S(2)}) copy-start(f32[512,64]{1,0:T(8,128)} %get-tuple-element.62) | copy-start | bytes 393220
  88.6 10.0 %copy-start.5 = (f32[512,64]{1,0:T(8,128)S(1)}, f32[512,64]{1,0:T(8,128)}, u32[]{:S(2)}) copy-start(f32[512,64]{1,0:T(8,128)} %get-tuple-element.63) | copy-start | bytes 393220
  88.6 10.0 %copy-start.6 = (f32[512,64]{1,0:T(8,128)S(1)}, f32[512,64]{1,0:T(8,128)}, u32[]{:S(2)}) copy-start(f32[512,64]{1,0:T(8,128)} %get-tuple-element.64) | copy-start | bytes 393220
  91.4 26.6 %all-to-all-start.2 = ((bf16[128,2,384]{2,1,0:T(2,128)(2,1)}), bf16[128,2,384]{2,1,0:T(2,128)(2,1)}, u32[]{:S(2)}, u32[]{:S(2)}) async-start(bf16[128,2,384]{2,1,0:T(2,128)(2,1)} %broadcast_in_dim.42), calls=%async_computation.2 | async-start | bytes 393216 | tf_op jit(solution)/shard_map/all_to_all | solution.py:154
  100.1 19.9 %copy-start.13 = (pred[128]{0:T(512)(128)(4,1)S(1)}, pred[128]{0:T(512)(128)(4,1)}, u32[]{:S(2)}) copy-start(pred[128]{0:T(512)(128)(4,1)} %get-tuple-element.100) | copy-start | bytes 388
  100.1 19.9 %copy-start.14 = (pred[128]{0:T(512)(128)(4,1)S(1)}, pred[128]{0:T(512)(128)(4,1)}, u32[]{:S(2)}) copy-start(pred[128]{0:T(512)(128)(4,1)} %get-tuple-element.101) | copy-start | bytes 388
  100.1 14.3 %collective-permute-start.4 = (bf16[256,256]{1,0:T(8,128)(2,1)S(1)}, bf16[256,256]{1,0:T(8,128)(2,1)S(1)}, u32[]{:S(2)}, u32[]{:S(2)}) collective-permute-start(bf16[256,256]{1,0:T(8,128)(2,1)S(1)} %get-tuple-element.52), channel_id=1, source_target_pairs={{0,127},{1,0},{2,1},{3,2},{4,3},{5,4},{6,5},{7,6},{8,7},{9,8},{10,... | collective-permute-start | bytes 393224 | tf_op jit(solution)/shard_map/ppermute | solution.py:15
  106.9 9.6 %collective-permute-start.3 = (bf16[256,256]{1,0:T(8,128)(2,1)S(1)}, bf16[256,256]{1,0:T(8,128)(2,1)S(1)}, u32[]{:S(2)}, u32[]{:S(2)}) collective-permute-start(bf16[256,256]{1,0:T(8,128)(2,1)S(1)} %get-tuple-element.51), channel_id=1, source_target_pairs={{0,1},{1,2},{2,3},{3,4},{4,5},{5,6},{6,7},{7,8},{8,9},{9,10},{10,1... | collective-permute-start | bytes 393224 | tf_op jit(solution)/shard_map/ppermute | solution.py:15
  116.6 0.8 copy-start.3
  117.4 12.3 %copy-start.11 = (s32[512]{0:T(512)S(1)}, s32[512]{0:T(512)}, u32[]{:S(2)}) copy-start(s32[512]{0:T(512)} %broadcast_bitcast_fusion) | copy-start | bytes 6148
  119.1 1.9 %copy-start.7 = (bf16[256,384]{1,0:T(8,128)(2,1)}, bf16[256,384]{1,0:T(8,128)(2,1)S(1)}, u32[]{:S(2)}) copy-start(bf16[256,384]{1,0:T(8,128)(2,1)S(1)} %reshape.162) | copy-start | bytes 589828
  120.9 20.5 %all-to-all-start.3 = ((bf16[128,2,256]{2,1,0:T(2,128)(2,1)}), bf16[128,2,256]{2,1,0:T(2,128)(2,1)}, u32[]{:S(2)}, u32[]{:S(2)}) async-start(bf16[128,2,256]{2,1,0:T(2,128)(2,1)} %reshape.163), calls=%async_computation.3 | async-start | bytes 262144 | tf_op jit(solution)/shard_map/all_to_all | solution.py:179
  129.6 2.0 %copy-start.8 = (bf16[256,384]{1,0:T(8,128)(2,1)S(1)}, bf16[256,384]{1,0:T(8,128)(2,1)}, u32[]{:S(2)}) copy-start(bf16[256,384]{1,0:T(8,128)(2,1)} %copy-done.7) | copy-start | bytes 589828
  132.0 0.8 copy-start.2
  132.8 19.2 %slice-start = ((bf16[256,384]{1,0:T(8,128)(2,1)}), bf16[256,128]{1,0:T(8,128)(2,1)S(1)}, s32[]{:S(2)}) async-start(bf16[256,384]{1,0:T(8,128)(2,1)} %copy-done.7), calls=%async_computation.5 | async-start | bytes 131072 | tf_op jit(solution)/shard_map/slice | solution.py:162
  145.9 17.2 %all-to-all-start.4 = ((bf16[128,2,128]{2,1,0:T(2,128)(2,1)}), bf16[128,2,128]{2,1,0:T(2,128)(2,1)S(1)}, u32[]{:S(2)}, u32[]{:S(2)}) async-start(bf16[128,2,128]{2,1,0:T(2,128)(2,1)} %broadcast_in_dim.46), calls=%async_computation.4 | async-start | bytes 131072 | tf_op jit(solution)/shard_map/all_to_all | solution.py:184
where the time goes:
time: 180 us; the launch traced here: 179 us
  starting transfers between devices  64.9 us (36%)
  waiting for transfers between devices  45.4 us (25%)
  other arithmetic  17.1 us (10%)
  local copies, waits for them, and re-layouts  14.5 us (8%)
  blocking collectives  14.4 us (8%)
  matrix products  12.9 us (7%)
  between operations  10.1 us (6%)
    ppermute x5, starting transfers between devices, shift(): lax.ppermute(value, axis, [(i, (i + by) % count) for i in range(count)])  22.3 us
    all_to_all x1, waiting for transfers between devices, on_device(): arrived = lax.all_to_all(jnp.stack(chunks), 'section', 0, 0)  16.7 us
    all_to_all x1, starting transfers between devices, on_device(): spread = lax.all_to_all(candidates, 'seq', 0, 0)  15.4 us
    all_gather x1, blocking collectives, on_device(): gathered = lax.all_gather(attended, 'section', axis=1, tiled=True)  14.4 us
    all_to_all x1, waiting for transfers between devices, on_device(): lax.all_to_all(jnp.broadcast_to(header_result.astype(bf16)[None], (shards...  9.42 us
    all_to_all x1, starting transfers between devices, on_device(): lax.all_to_all(partial.reshape(shards, mine, 2 * head_width), 'seq', 0, 0)  8.69 us
    all_to_all x1, waiting for transfers between devices, on_device(): lax.all_to_all(partial.reshape(shards, mine, 2 * head_width), 'seq', 0, 0)  8.1 us
    all_to_all x1, waiting for transfers between devices, on_device(): spread = lax.all_to_all(candidates, 'seq', 0, 0)  7.9 us
  transfers between devices with their start and end apart: 10, of which 6 were waited for; matrix products, arithmetic and copies ran while one was open for 10% of the time, Pallas kernels for 0%

commit v1 on v0

--- a/solution.py
+++ b/solution.py
@@ -8,6 +8,11 @@
 REACH = 2
 EPSILON = 1e-05
 THETA = 500000.0
+
+
+def all_by_exchange(x, mesh_axis, dim):
+    sent = jnp.stack([x] * lax.axis_size(mesh_axis))
+    return jnp.concatenate(lax.all_to_all(sent, mesh_axis, 0, 0), axis=dim)
 
 
 def shift(value, axis, by):
@@ -225,7 +230,7 @@
             block = jnp.where(here, header_all[:, h].reshape(BLOCK, head_width), block)
         blocks.append(block)
     attended = jnp.concatenate(blocks, axis=0)
-    gathered = lax.all_gather(attended, "section", axis=1, tiled=True)
+    gathered = all_by_exchange(attended, "section", 1)
     return jnp.dot(gathered, output_weight, preferred_element_type=f32).astype(bf16)
 
 

time: 180 us -> 179 us (level)
  the two profiles are of different devices: /device:TPU:2 before, /device:TPU:1 now
where the time goes in v1:
time: 179 us; the launch traced here: 178 us
  starting transfers between devices  64.7 us (36%)
  waiting for transfers between devices  47.5 us (27%)
  other arithmetic  17.1 us (10%)
  local copies, waits for them, and re-layouts  14.6 us (8%)
  matrix products  12.9 us (7%)
  blocking collectives  11.4 us (6%)
  between operations  10.1 us (6%)
    all_to_all x1, starting transfers between devices, on_device(): spread = lax.all_to_all(candidates, 'seq', 0, 0)  18.6 us
    all_to_all x1, waiting for transfers between devices, on_device(): arrived = lax.all_to_all(jnp.stack(chunks), 'section', 0, 0)  17.3 us
    ppermute x5, starting transfers between devices, shift(): lax.ppermute(value, axis, [(i, (i + by) % count) for i in range(count)])  15.9 us
    all_to_all x1, starting transfers between devices, on_device(): lax.all_to_all(partial.reshape(shards, mine, 2 * head_width), 'seq', 0, 0)  14.1 us
    all_to_all x1, blocking collectives, all_by_exchange(): return jnp.concatenate(lax.all_to_all(sent, mesh_axis, 0, 0), axis=dim)  11.4 us
    all_to_all x1, waiting for transfers between devices, on_device(): lax.all_to_all(jnp.broadcast_to(header_result.astype(bf16)[None], (shards...  9.86 us
    all_to_all x1, waiting for transfers between devices, on_device(): spread = lax.all_to_all(candidates, 'seq', 0, 0)  8.98 us
    all_to_all x1, waiting for transfers between devices, on_device(): lax.all_to_all(partial.reshape(shards, mine, 2 * head_width), 'seq', 0, 0)  8.68 us
  transfers between devices with their start and end apart: 10, of which 5 were waited for; matrix products, arithmetic and copies ran while one was open for 10% of the time, Pallas kernels for 0%

profile of v1, /device:TPU:1, one launch (start us, length us, event | category | flops | bytes accessed | tf_op | source)
XLA Modules:
  0.0 178.3 jit_solution(3130387748480801755)
XLA Ops:
  0.1 1.6 fusion.1
  1.7 1.2 constant_dynamic-slice_fusion.2
  3.0 5.2 %collective-permute-start.2 = (bf16[1032,128]{1,0:T(8,128)(2,1)S(1)}, bf16[1032,128]{1,0:T(8,128)(2,1)}, u32[]{:S(2)}, u32[]{:S(2)}) collective-permute-start(bf16[1032,128]{1,0:T(8,128)(2,1)S(1)} %concatenate.78), channel_id=1, source_target_pairs={{0,384},{128,0},{256,128},{384,256},{1,385},{129,1},{257,129},{385... | collective-permute-start | bytes 792584 | tf_op jit(solution)/shard_map/ppermute | solution.py:20
  8.4 2.4 %collective-permute-start.1 = (bf16[1032,128]{1,0:T(8,128)(2,1)S(1)}, bf16[1032,128]{1,0:T(8,128)(2,1)}, u32[]{:S(2)}, u32[]{:S(2)}) collective-permute-start(bf16[1032,128]{1,0:T(8,128)(2,1)S(1)} %concatenate.77), channel_id=1, source_target_pairs={{0,256},{128,384},{256,0},{384,128},{1,257},{129,385},{257,1},{385... | collective-permute-start | bytes 792584 | tf_op jit(solution)/shard_map/ppermute | solution.py:20
  13.3 1.3 copy.31
  14.6 18.6 %all-to-all-start = ((bf16[128,2,1024]{2,1,0:T(2,128)(2,1)}), bf16[128,2,1024]{2,1,0:T(2,128)(2,1)}, u32[]{:S(2)}, u32[]{:S(2)}) async-start(bf16[128,2,1024]{2,1,0:T(2,128)(2,1)} %copy.31), calls=%async_computation | async-start | bytes 1048576 | tf_op jit(solution)/shard_map/all_to_all | solution.py:81
  33.4 2.5 %collective-permute-start = (bf16[1032,128]{1,0:T(8,128)(2,1)S(1)}, bf16[1032,128]{1,0:T(8,128)(2,1)}, u32[]{:S(2)}, u32[]{:S(2)}) collective-permute-start(bf16[1032,128]{1,0:T(8,128)(2,1)S(1)} %concatenate.76), channel_id=1, source_target_pairs={{0,128},{128,256},{256,384},{384,0},{1,129},{129,257},{257,385},{3... | collective-permute-start | bytes 792584 | tf_op jit(solution)/shard_map/ppermute | solution.py:20
  39.5 0.7 slice_convert_fusion.7
  40.2 0.7 slice_convert_fusion.8
  40.8 2.6 %collective-permute-done = bf16[1032,128]{1,0:T(8,128)(2,1)} collective-permute-done((bf16[1032,128]{1,0:T(8,128)(2,1)S(1)}, bf16[1032,128]{1,0:T(8,128)(2,1)}, u32[]{:S(2)}, u32[]{:S(2)}) %collective-permute-start) | collective-permute-done | bytes 264224 | tf_op jit(solution)/shard_map/ppermute | solution.py:20
  43.5 0.7 slice_convert_fusion.9
  44.5 9.0 %all-to-all-done = bf16[128,2,1024]{2,1,0:T(2,128)(2,1)} async-done(((bf16[128,2,1024]{2,1,0:T(2,128)(2,1)}), bf16[128,2,1024]{2,1,0:T(2,128)(2,1)}, u32[]{:S(2)}, u32[]{:S(2)}) %all-to-all-start) | async-done | bytes 524320 | tf_op jit(solution)/shard_map/all_to_all | solution.py:81
  53.5 0.7 dynamic-slice_bitcast_fusion.3
  54.3 1.4 fusion.35
  55.7 1.4 fusion.28
  57.1 1.4 fusion.30
  58.5 1.4 fusion.32
  62.4 1.4 pad_maximum_fusion
  63.9 3.8 %all-to-all-start.1 = ((bf16[4,1664,128]{2,1,0:T(8,128)(2,1)}), bf16[4,1664,128]{2,1,0:T(8,128)(2,1)S(1)}, u32[]{:S(2)}, u32[]{:S(2)}) async-start(bf16[4,1664,128]{2,1,0:T(8,128)(2,1)} %pad_maximum_fusion), calls=%async_computation.1 | async-start | bytes 3407872 | tf_op jit(solution)/shard_map/all_to_all | solution.py:146
  68.9 0.7 compare_reduce_fusion
  70.2 0.7 fusion.84
  70.9 1.9 %fusion.39 = (f32[512,64]{1,0:T(8,128)}, f32[512,64]{1,0:T(8,128)}, f32[512,64]{1,0:T(8,128)}) fusion(f32[64]{0:T(128)S(1)} %multiply_exponential_fusion, f32[512]{0:T(512)S(1)} %add_convert_fusion), kind=kLoop, calls=%fused_computation.79 | loop fusion | flops 65536 | bytes 395520 | tf_op jit(solution)/shard_map/neg | solution.py:30
  72.8 17.3 %all-to-all-done.1 = bf16[4,1664,128]{2,1,0:T(8,128)(2,1)S(1)} async-done(((bf16[4,1664,128]{2,1,0:T(8,128)(2,1)}), bf16[4,1664,128]{2,1,0:T(8,128)(2,1)S(1)}, u32[]{:S(2)}, u32[]{:S(2)}) %all-to-all-start.1) | async-done | bytes 1703968 | tf_op jit(solution)/shard_map/all_to_all | solution.py:146
  90.4 0.9 fusion.95
  91.5 0.8 fusion.70
  92.4 0.8 broadcast_in_dim.42
  93.2 6.8 %all-to-all-start.2 = ((bf16[128,2,384]{2,1,0:T(2,128)(2,1)}), bf16[128,2,384]{2,1,0:T(2,128)(2,1)}, u32[]{:S(2)}, u32[]{:S(2)}) async-start(bf16[128,2,384]{2,1,0:T(2,128)(2,1)} %broadcast_in_dim.42), calls=%async_computation.2 | async-start | bytes 393216 | tf_op jit(solution)/shard_map/all_to_all | solution.py:159
  100.0 1.4 fusion.25
  101.5 3.0 %collective-permute-start.4 = (bf16[256,256]{1,0:T(8,128)(2,1)S(1)}, bf16[256,256]{1,0:T(8,128)(2,1)S(1)}, u32[]{:S(2)}, u32[]{:S(2)}) collective-permute-start(bf16[256,256]{1,0:T(8,128)(2,1)S(1)} %get-tuple-element.52), channel_id=1, source_target_pairs={{0,127},{1,0},{2,1},{3,2},{4,3},{5,4},{6,5},{7,6},{8,7},{9,8},{10,... | collective-permute-start | bytes 393224 | tf_op jit(solution)/shard_map/ppermute | solution.py:20
  104.5 2.8 %collective-permute-start.3 = (bf16[256,256]{1,0:T(8,128)(2,1)S(1)}, bf16[256,256]{1,0:T(8,128)(2,1)S(1)}, u32[]{:S(2)}, u32[]{:S(2)}) collective-permute-start(bf16[256,256]{1,0:T(8,128)(2,1)S(1)} %get-tuple-element.51), channel_id=1, source_target_pairs={{0,1},{1,2},{2,3},{3,4},{4,5},{5,6},{6,7},{7,8},{8,9},{9,10},{10,1... | collective-permute-start | bytes 393224 | tf_op jit(solution)/shard_map/ppermute | solution.py:20
  111.9 0.7 not.7
  112.7 0.8 copy-done.3
  113.5 0.7 slice.376
  114.2 1.0 reshape.170
  116.3 0.7 reshape.171
  117.0 14.1 %all-to-all-start.3 = ((bf16[128,2,256]{2,1,0:T(2,128)(2,1)}), bf16[128,2,256]{2,1,0:T(2,128)(2,1)}, u32[]{:S(2)}, u32[]{:S(2)}) async-start(bf16[128,2,256]{2,1,0:T(2,128)(2,1)} %reshape.171), calls=%async_computation.3 | async-start | bytes 262144 | tf_op jit(solution)/shard_map/all_to_all | solution.py:184
  131.1 2.0 %fusion.102 = (f32[512]{0:T(512)S(1)}, f32[512,1024]{1,0:T(8,128)S(1)}) fusion(bf16[512,128]{1,0:T(8,128)(2,1)S(1)} %get-tuple-element.8, bf16[1024,256]{1,0:T(8,128)(2,1)} %copy-done.3, pred[1024]{0:T(1024)(128)(4,1)S(1)} %not.7, s32[512]{0:T(512)S(1)} %copy-done.11, s32[512]{0:T(512)S(1)} %fusion.54, s32[1024]{0:T(1024)S(1)} %fusion.50, ...), kind=kOutput, calls=%fused_computation.232 | convolution fusion | flops 138411520 | bytes 2502656 | tf_op jit(solution)/shard_map/qd,kd->qk/dot_general | solution.py:211
  133.5 0.8 copy-done.2
  134.8 8.7 %all-to-all-done.3 = bf16[128,2,256]{2,1,0:T(2,128)(2,1)} async-done(((bf16[128,2,256]{2,1,0:T(2,128)(2,1)}), bf16[128,2,256]{2,1,0:T(2,128)(2,1)}, u32[]{:S(2)}, u32[]{:S(2)}) %all-to-all-start.3) | async-done | bytes 131104 | tf_op jit(solution)/shard_map/all_to_all | solution.py:184
  143.5 1.0 convert_element_type.263
  144.9 0.9 fusion.87
  145.9 1.0 copy.33
  147.3 0.7 broadcast_in_dim.46
  147.9 5.5 %all-to-all-start.4 = ((bf16[128,2,128]{2,1,0:T(2,128)(2,1)}), bf16[128,2,128]{2,1,0:T(2,128)(2,1)S(1)}, u32[]{:S(2)}, u32[]{:S(2)}) async-start(bf16[128,2,128]{2,1,0:T(2,128)(2,1)} %broadcast_in_dim.46), calls=%async_computation.4 | async-start | bytes 131072 | tf_op jit(solution)/shard_map/all_to_all | solution.py:189
  153.4 1.7 fusion.13
  155.1 9.9 %all-to-all-done.4 = bf16[128,2,128]{2,1,0:T(2,128)(2,1)S(1)} async-done(((bf16[128,2,128]{2,1,0:T(2,128)(2,1)}), bf16[128,2,128]{2,1,0:T(2,128)(2,1)S(1)}, u32[]{:S(2)}, u32[]{:S(2)}) %all-to-all-start.4) | async-done | bytes 65568 | tf_op jit(solution)/shard_map/all_to_all | solution.py:189
  165.2 11.4 %all_to_all.30 = bf16[4,512,128]{1,2,0:T(8,128)(2,1)S(1)} all-to-all(bf16[4,512,128]{1,2,0:T(8,128)(2,1)S(1)} %stack.27), channel_id=1, replica_groups=mesh['section'=4,'seq'=128] {'section'}, dimensions={0} | all-to-all | bytes 1048576 | tf_op jit(solution)/shard_map/all_to_all | solution.py:15
  176.6 1.7 convolution_convert_fusion
  (115 shorter events, 9.9 us)
Async XLA Ops:
  0.0 176.6 %copy-start = (bf16[512,1024]{1,0:T(8,128)(2,1)S(1)}, bf16[512,1024]{1,0:T(8,128)(2,1)}, u32[]{:S(2)}) copy-start(bf16[512,1024]{1,0:T(8,128)(2,1)} %param.13) | copy-start | bytes 3145732
  0.0 13.1 %copy-start.1 = (bf16[512,1024]{1,0:T(8,128)(2,1)S(1)}, bf16[512,1024]{1,0:T(8,128)(2,1)}, u32[]{:S(2)}) copy-start(bf16[512,1024]{1,0:T(8,128)(2,1)} %param.8) | copy-start | bytes 3145732
  0.0 10.8 %copy-start.9 = (s32[2]{0:T(128)S(1)}, s32[2]{0:T(128)}, u32[]{:S(2)}) copy-start(s32[2]{0:T(128)} %param.15) | copy-start | bytes 28
  3.0 36.4 %collective-permute-start.2 = (bf16[1032,128]{1,0:T(8,128)(2,1)S(1)}, bf16[1032,128]{1,0:T(8,128)(2,1)}, u32[]{:S(2)}, u32[]{:S(2)}) collective-permute-start(bf16[1032,128]{1,0:T(8,128)(2,1)S(1)} %concatenate.78), channel_id=1, source_target_pairs={{0,384},{128,0},{256,128},{384,256},{1,385},{129,1},{257,129},{385... | collective-permute-start | bytes 792584 | tf_op jit(solution)/shard_map/ppermute | solution.py:20
  8.4 31.8 %collective-permute-start.1 = (bf16[1032,128]{1,0:T(8,128)(2,1)S(1)}, bf16[1032,128]{1,0:T(8,128)(2,1)}, u32[]{:S(2)}, u32[]{:S(2)}) collective-permute-start(bf16[1032,128]{1,0:T(8,128)(2,1)S(1)} %concatenate.77), channel_id=1, source_target_pairs={{0,256},{128,384},{256,0},{384,128},{1,257},{129,385},{257,1},{385... | collective-permute-start | bytes 792584 | tf_op jit(solution)/shard_map/ppermute | solution.py:20
  13.2 25.1 %copy-start.10 = (bf16[1024]{0:T(1024)(128)(2,1)S(1)}, bf16[1024]{0:T(1024)(128)(2,1)}, u32[]{:S(2)}) copy-start(bf16[1024]{0:T(1024)(128)(2,1)} %param.9) | copy-start | bytes 6148
  14.6 38.8 %all-to-all-start = ((bf16[128,2,1024]{2,1,0:T(2,128)(2,1)}), bf16[128,2,1024]{2,1,0:T(2,128)(2,1)}, u32[]{:S(2)}, u32[]{:S(2)}) async-start(bf16[128,2,1024]{2,1,0:T(2,128)(2,1)} %copy.31), calls=%async_computation | async-start | bytes 1048576 | tf_op jit(solution)/shard_map/all_to_all | solution.py:81
  33.4 10.1 %collective-permute-start = (bf16[1032,128]{1,0:T(8,128)(2,1)S(1)}, bf16[1032,128]{1,0:T(8,128)(2,1)}, u32[]{:S(2)}, u32[]{:S(2)}) collective-permute-start(bf16[1032,128]{1,0:T(8,128)(2,1)S(1)} %concatenate.76), channel_id=1, source_target_pairs={{0,128},{128,256},{256,384},{384,0},{1,129},{129,257},{257,385},{3... | collective-permute-start | bytes 792584 | tf_op jit(solution)/shard_map/ppermute | solution.py:20
  58.5 1.6 copy-start.16
  60.1 1.0 copy-start.17
  63.9 5.7 %copy-start.15 = (s32[4]{0:T(128)S(1)}, s32[4]{0:T(128)}, u32[]{:S(2)}) copy-start(s32[4]{0:T(128)} %param.14) | copy-start | bytes 52
  63.9 6.3 %copy-start.12 = (f32[2]{0:T(128)S(1)}, f32[2]{0:T(128)}, u32[]{:S(2)}) copy-start(f32[2]{0:T(128)} %get-tuple-element.83) | copy-start | bytes 28
  63.9 26.2 %all-to-all-start.1 = ((bf16[4,1664,128]{2,1,0:T(8,128)(2,1)}), bf16[4,1664,128]{2,1,0:T(8,128)(2,1)S(1)}, u32[]{:S(2)}, u32[]{:S(2)}) async-start(bf16[4,1664,128]{2,1,0:T(8,128)(2,1)} %pad_maximum_fusion), calls=%async_computation.1 | async-start | bytes 3407872 | tf_op jit(solution)/shard_map/all_to_all | solution.py:146
  90.3 9.6 %copy-start.4 = (f32[512,64]{1,0:T(8,128)S(1)}, f32[512,64]{1,0:T(8,128)}, u32[]{:S(2)}) copy-start(f32[512,64]{1,0:T(8,128)} %get-tuple-element.62) | copy-start | bytes 393220
  90.4 9.6 %copy-start.5 = (f32[512,64]{1,0:T(8,128)S(1)}, f32[512,64]{1,0:T(8,128)}, u32[]{:S(2)}) copy-start(f32[512,64]{1,0:T(8,128)} %get-tuple-element.63) | copy-start | bytes 393220
  90.4 9.6 %copy-start.6 = (f32[512,64]{1,0:T(8,128)S(1)}, f32[512,64]{1,0:T(8,128)}, u32[]{:S(2)}) copy-start(f32[512,64]{1,0:T(8,128)} %get-tuple-element.64) | copy-start | bytes 393220
  93.2 21.0 %all-to-all-start.2 = ((bf16[128,2,384]{2,1,0:T(2,128)(2,1)}), bf16[128,2,384]{2,1,0:T(2,128)(2,1)}, u32[]{:S(2)}, u32[]{:S(2)}) async-start(bf16[128,2,384]{2,1,0:T(2,128)(2,1)} %broadcast_in_dim.42), calls=%async_computation.2 | async-start | bytes 393216 | tf_op jit(solution)/shard_map/all_to_all | solution.py:159
  101.4 14.6 %copy-start.13 = (pred[128]{0:T(512)(128)(4,1)S(1)}, pred[128]{0:T(512)(128)(4,1)}, u32[]{:S(2)}) copy-start(pred[128]{0:T(512)(128)(4,1)} %get-tuple-element.100) | copy-start | bytes 388
  101.5 14.6 %copy-start.14 = (pred[128]{0:T(512)(128)(4,1)S(1)}, pred[128]{0:T(512)(128)(4,1)}, u32[]{:S(2)}) copy-start(pred[128]{0:T(512)(128)(4,1)} %get-tuple-element.101) | copy-start | bytes 388
  101.5 11.1 %collective-permute-start.4 = (bf16[256,256]{1,0:T(8,128)(2,1)S(1)}, bf16[256,256]{1,0:T(8,128)(2,1)S(1)}, u32[]{:S(2)}, u32[]{:S(2)}) collective-permute-start(bf16[256,256]{1,0:T(8,128)(2,1)S(1)} %get-tuple-element.52), channel_id=1, source_target_pairs={{0,127},{1,0},{2,1},{3,2},{4,3},{5,4},{6,5},{7,6},{8,7},{9,8},{10,... | collective-permute-start | bytes 393224 | tf_op jit(solution)/shard_map/ppermute | solution.py:20
  104.5 8.1 %collective-permute-start.3 = (bf16[256,256]{1,0:T(8,128)(2,1)S(1)}, bf16[256,256]{1,0:T(8,128)(2,1)S(1)}, u32[]{:S(2)}, u32[]{:S(2)}) collective-permute-start(bf16[256,256]{1,0:T(8,128)(2,1)S(1)} %get-tuple-element.51), channel_id=1, source_target_pairs={{0,1},{1,2},{2,3},{3,4},{4,5},{5,6},{6,7},{7,8},{8,9},{9,10},{10,1... | collective-permute-start | bytes 393224 | tf_op jit(solution)/shard_map/ppermute | solution.py:20
  112.7 0.8 copy-start.3
  113.5 17.6 %copy-start.11 = (s32[512]{0:T(512)S(1)}, s32[512]{0:T(512)}, u32[]{:S(2)}) copy-start(s32[512]{0:T(512)} %broadcast_bitcast_fusion) | copy-start | bytes 6148
  115.2 1.9 %copy-start.7 = (bf16[256,384]{1,0:T(8,128)(2,1)}, bf16[256,384]{1,0:T(8,128)(2,1)S(1)}, u32[]{:S(2)}) copy-start(bf16[256,384]{1,0:T(8,128)(2,1)S(1)} %reshape.170) | copy-start | bytes 589828
  117.0 26.4 %all-to-all-start.3 = ((bf16[128,2,256]{2,1,0:T(2,128)(2,1)}), bf16[128,2,256]{2,1,0:T(2,128)(2,1)}, u32[]{:S(2)}, u32[]{:S(2)}) async-start(bf16[128,2,256]{2,1,0:T(2,128)(2,1)} %reshape.171), calls=%async_computation.3 | async-start | bytes 262144 | tf_op jit(solution)/shard_map/all_to_all | solution.py:184
  131.1 2.0 %copy-start.8 = (bf16[256,384]{1,0:T(8,128)(2,1)S(1)}, bf16[256,384]{1,0:T(8,128)(2,1)}, u32[]{:S(2)}) copy-start(bf16[256,384]{1,0:T(8,128)(2,1)} %copy-done.7) | copy-start | bytes 589828
  133.5 0.8 copy-start.2
  134.3 19.1 %slice-start = ((bf16[256,384]{1,0:T(8,128)(2,1)}), bf16[256,128]{1,0:T(8,128)(2,1)S(1)}, s32[]{:S(2)}) async-start(bf16[256,384]{1,0:T(8,128)(2,1)} %copy-done.7), calls=%async_computation.6 | async-start | bytes 131072 | tf_op jit(solution)/shard_map/slice | solution.py:167
  147.9 17.0 %all-to-all-start.4 = ((bf16[128,2,128]{2,1,0:T(2,128)(2,1)}), bf16[128,2,128]{2,1,0:T(2,128)(2,1)S(1)}, u32[]{:S(2)}, u32[]{:S(2)}) async-start(bf16[128,2,128]{2,1,0:T(2,128)(2,1)} %broadcast_in_dim.46), calls=%async_computation.4 | async-start | bytes 131072 | tf_op jit(solution)/shard_map/all_to_all | solution.py:189
